TPU v7x, 32 devices: a whole 2x2x4 slice. The times are simulated.
32 devices in a mesh: seq: 8 (over z, core), tp: 4 (over y, x).
Axes of the slice: x: 2, y: 2, z: 4, core: 2. Of those that a mesh axis runs over, the one named last changes fastest.
Arguments:
- features: bfloat16 [3, 2048, 8192], P(None, 'seq', 'tp'), may hold values from -6 to 6
- short_filter: float32 [7, 3, 8192], P(None, None, 'tp'), may hold values from -2 to 2
- medium_filter: float32 [128, 8192], P('seq', 'tp'), may hold values from -0.5 to 0.5
- skip_gain: float32 [8192], P('tp'), may hold values from -4 to 4
- out_weight: bfloat16 [8192, 8192], P(None, 'tp'), may hold values from -0.0625 to 0.0625
Outputs:
- block_out: bfloat16 [2048, 8192], P('seq', 'tp')
All inputs are finite; a program needn't handle non-finite values.
Results may differ from a plain program's by a relative error of at most 0.0058.
Values may be sent and summed in bfloat16 or wider, within the bound.
A program may use at most 128 MiB of HBM per device.

v0:
```python
import functools

import jax
import jax.numpy as jnp
import ml_dtypes
import numpy as np
from jax import lax
from jax.experimental import pallas as pl
from jax.experimental.pallas import tpu as pltpu
from jax.sharding import PartitionSpec as P

MESH = pl.DeviceIdType.MESH
F32 = jnp.float32
BF16 = jnp.bfloat16


def passed_along(value, axis, steps):
    count = lax.axis_size(axis)
    leading, last = (max(0, -steps), min(count, count - steps))
    return lax.ppermute(value, axis, [(source, source + steps) for source in range(leading, last)])


def depthwise(extended, kernel):
    channels = extended.shape[1]
    return lax.conv_general_dilated(
        extended[None],
        kernel[::-1][:, None, :],
        (1,),
        "VALID",
        dimension_numbers=("NWC", "WIO", "NWC"),
        feature_group_count=channels,
        precision=lax.Precision.HIGHEST,
    )[0]


def on_device(features, short_filter, medium_filter, skip_gain, out_weight):
    taps_full = lax.all_gather(medium_filter, "seq", axis=0, tiled=True)
    long_reach = taps_full.shape[0]
    short_reach = short_filter.shape[0]
    tok_rows = features.shape[1]
    lead_rows = passed_along(features[:, tok_rows - (short_reach - 1) :, :], "seq", 1)
    extended = jnp.concatenate([lead_rows, features], 1).astype(F32)
    query_conv = depthwise(extended[0], short_filter[:, 0, :])
    key_conv = depthwise(extended[1], short_filter[:, 1, :])
    value_conv = depthwise(extended[2], short_filter[:, 2, :])
    product = (key_conv * value_conv).astype(BF16)
    lead_product = passed_along(product[tok_rows - (long_reach - 1) :], "seq", 1)
    product_ext = jnp.concatenate([lead_product, product], 0)
    longer = depthwise(product_ext.astype(F32), taps_full)
    gated_rows = (query_conv * (longer + skip_gain * product.astype(F32))).astype(BF16)
    gathered = lax.all_gather(gated_rows, "tp", axis=1, tiled=True)
    result = jnp.dot(gathered, out_weight, preferred_element_type=F32)
    return result.astype(BF16)


def split(matrix):
    high = matrix.astype(ml_dtypes.bfloat16)
    low = (matrix - high.astype(np.float64)).astype(ml_dtypes.bfloat16)
    return np.stack([high, low])


def transforms(points):
    half = points // 2
    at = np.arange(points)
    angle = 2 * np.pi * ((np.arange(half)[:, None] * at[None, :]) % points) / points
    real, imag = np.cos(angle), -np.sin(angle)
    imag[0] = np.where(at % 2 == 0, 1.0, -1.0)
    forward = np.concatenate([real, imag], 0)
    weight = np.full((points, 1), 2.0 / points)
    weight[0] = weight[half] = 1.0 / points
    inverse = (forward * weight).T[half:]
    return split(forward), split(inverse)


def dot(a, b):
    return jnp.dot(a, b, preferred_element_type=F32)


def kernel(
    sizes,
    features,
    short_ref,
    medium_ref,
    skip_ref,
    forward_ref,
    inverse_ref,
    weight,
    out_ref,
    feat,
    fhalo,
    ext,
    query,
    prod,
    phalo,
    taps,
    gath,
    wbuf,
    acc,
    feat_sem,
    w_sem,
    fh_send,
    fh_recv,
    ph_send,
    ph_recv,
    tap_send,
    tap_recv,
    g_send,
    g_recv,
    d_send,
    d_recv,
):
    seqs, tps, chunks, width, rows, channels, own_taps, short = sizes
    half = rows // 2
    edge = 16
    s = lax.axis_index("seq")
    p = lax.axis_index("tp")
    beside = (p + 1 - 2 * lax.rem(p, 2), lax.rem(p + 2, 4))
    across = 3 - p

    def feat_copy(c):
        return pltpu.make_async_copy(
            features.at[:, :, pl.ds(pl.multiple_of(c * width, width), width)],
            feat.at[c],
            feat_sem.at[c],
        )

    def w_copy(q, c):
        first = pl.multiple_of(q * channels + c * width, width)
        return pltpu.make_async_copy(
            weight.at[pl.ds(first, width), :], wbuf.at[q, c], w_sem.at[q, c]
        )

    def fh_copy(c):
        return pltpu.make_async_remote_copy(
            src_ref=feat.at[c, :, pl.ds(rows - edge, edge), :],
            dst_ref=fhalo.at[c],
            send_sem=fh_send.at[c],
            recv_sem=fh_recv.at[c],
            device_id=(s + 1, p),
            device_id_type=MESH,
        )

    def ph_copy(c):
        return pltpu.make_async_remote_copy(
            src_ref=prod.at[c, pl.ds(half, half), :],
            dst_ref=phalo.at[c],
            send_sem=ph_send.at[c],
            recv_sem=ph_recv.at[c],
            device_id=(s + 1, p),
            device_id_type=MESH,
        )

    def tap_copy(c, k):
        mine = pl.ds(pl.multiple_of(s * own_taps, own_taps), own_taps)
        return pltpu.make_async_remote_copy(
            src_ref=taps.at[c, mine, :],
            dst_ref=taps.at[c, mine, :],
            send_sem=tap_send.at[c, k - 1],
            recv_sem=tap_recv.at[c, k - 1],
            device_id=(lax.rem(s + k, seqs), p),
            device_id_type=MESH,
        )

    def tap_arrival(c, k):
        other = lax.rem(s + seqs - k, seqs)
        theirs = pl.ds(pl.multiple_of(other * own_taps, own_taps), own_taps)
        return pltpu.make_async_remote_copy(
            src_ref=taps.at[c, theirs, :],
            dst_ref=taps.at[c, theirs, :],
            send_sem=tap_send.at[c, k - 1],
            recv_sem=tap_recv.at[c, k - 1],
            device_id=(other, p),
            device_id_type=MESH,
        )

    def g_copy(owner, c, way):
        return pltpu.make_async_remote_copy(
            src_ref=gath.at[owner, c],
            dst_ref=gath.at[owner, c],
            send_sem=g_send.at[c, way],
            recv_sem=g_recv.at[c, way],
            device_id=(s, beside[way]),
            device_id_type=MESH,
        )

    def d_copy(owner, c, way):
        piece = pl.ds(way * half, half)
        return pltpu.make_async_remote_copy(
            src_ref=gath.at[owner, c, piece, :],
            dst_ref=gath.at[owner, c, piece, :],
            send_sem=d_send.at[c, way],
            recv_sem=d_recv.at[c, way],
            device_id=(s, beside[1 - way]),
            device_id_type=MESH,
        )

    for c in range(chunks):
        feat_copy(c).start()
    barrier = pltpu.get_barrier_semaphore()
    for k in range(1, seqs):
        pl.semaphore_signal(
            barrier, inc=1, device_id=(lax.rem(s + k, seqs), p), device_id_type=MESH
        )
    for way in range(2):
        pl.semaphore_signal(barrier, inc=1, device_id=(s, beside[way]), device_id_type=MESH)

    own = pl.ds(pl.multiple_of(s * own_taps, own_taps), own_taps)
    for c in range(chunks):
        taps[c, own, :] = medium_ref[:, c * width : (c + 1) * width].astype(BF16)

    @pl.when(s == 0)
    def _():
        fhalo[...] = jnp.zeros_like(fhalo)
        phalo[...] = jnp.zeros_like(phalo)

    acc[...] = jnp.zeros_like(acc)
    pl.semaphore_wait(barrier, seqs + 1)

    @pl.loop(0, chunks)
    def _(c):
        feat_copy(c).wait()

        @pl.when(s < seqs - 1)
        def _():
            fh_copy(c).start()

        for k in range(1, seqs):
            tap_copy(c, k).start()

    @pl.loop(0, chunks)
    def _(c):
        for q in range(tps):
            w_copy(q, c).start()

    def short_conv(c, stream):
        lanes = pl.ds(pl.multiple_of(c * width, width), width)
        ext[stream, 0:8, :] = fhalo[c, stream, :, :].astype(F32)[edge - 8 :]
        ext[stream, 8:, :] = feat[c, stream, :, :].astype(F32)
        total = None
        for j in range(short):
            term = short_ref[j, pl.ds(stream, 1), lanes] * ext[stream, pl.ds(8 - j, rows), :]
            total = term if total is None else total + term
        return total

    def products(c):
        @pl.when(s > 0)
        def _():
            fh_copy(c).wait_recv()

        prod[c] = (short_conv(c, 1) * short_conv(c, 2)).astype(BF16)

        @pl.when(s < seqs - 1)
        def _():
            ph_copy(c).start()

        query[lax.rem(c, 2)] = short_conv(c, 0)

    def gate(c):
        lanes = pl.ds(pl.multiple_of(c * width, width), width)
        for k in range(1, seqs):
            tap_arrival(c, k).wait_recv()
        f_high, f_low = forward_ref[0], forward_ref[1]
        i_high, i_low = inverse_ref[0], inverse_ref[1]
        h = taps[c]
        spectrum = dot(f_high[:, :half], h) + dot(f_low[:, :half], h)
        skip = skip_ref[pl.ds(0, 1), lanes]
        first = lax.broadcasted_iota(jnp.int32, (half, width), 0) == 0
        h_real = spectrum[:half] + skip
        h_imag = jnp.where(first, 0.0, spectrum[half:])
        h_last = jnp.where(first, spectrum[half:] + skip, h_real)

        def block(before, now):
            window = jnp.concatenate([before, now], 0)
            x = dot(f_high, window) + dot(f_low, window)
            a, b = x[:half], x[half:]
            y = jnp.concatenate([a * h_real - b * h_imag, a * h_imag + b * h_last], 0)
            y_high = y.astype(BF16)
            y_low = (y - y_high.astype(F32)).astype(BF16)
            return dot(i_high, y_high) + dot(i_low, y_high) + dot(i_high, y_low)

        slot = lax.rem(c, 2)
        upper = block(prod[c, 0:half, :], prod[c, half:, :])
        gath[p, c, pl.ds(half, half), :] = (query[slot, pl.ds(half, half), :] * upper).astype(BF16)

        @pl.when(s > 0)
        def _():
            ph_copy(c).wait_recv()

        lower = block(phalo[c], prod[c, 0:half, :])
        gath[p, c, pl.ds(0, half), :] = (query[slot, pl.ds(0, half), :] * lower).astype(BF16)
        for way in range(2):
            g_copy(p, c, way).start()

    def pass_on(c):
        for way in range(2):
            g_copy(beside[way], c, way).wait_recv()
            d_copy(beside[way], c, way).start()

    tile = 512

    def project(c):
        for way in range(2):
            d_copy(across, c, way).wait_recv()
        for q in range(tps):
            w_copy(q, c).wait()

        @pl.loop(0, channels // tile)
        def _(n):
            lanes = pl.ds(pl.multiple_of(n * tile, tile), tile)
            total = acc[:, lanes]
            for q in range(tps):
                total = total + dot(gath[q, c], wbuf[q, c, :, lanes])
            acc[:, lanes] = total

    lag = 3

    @pl.loop(0, chunks + lag)
    def _(i):
        @pl.when(i < chunks)
        def _():
            products(i)

        @pl.when((i >= 1) & (i < chunks + 1))
        def _():
            gate(i - 1)

        @pl.when((i >= 2) & (i < chunks + 2))
        def _():
            pass_on(i - 2)

        @pl.when(i >= lag)
        def _():
            project(i - lag)

    out_ref[...] = acc[...].astype(BF16)

    @pl.loop(0, chunks)
    def _(c):
        @pl.when(s < seqs - 1)
        def _():
            fh_copy(c).wait_send()
            ph_copy(c).wait_send()

        for k in range(1, seqs):
            tap_copy(c, k).wait_send()
        for way in range(2):
            g_copy(p, c, way).wait_send()
            d_copy(beside[way], c, way).wait_send()


def fused(seqs, tps, features, short_filter, medium_filter, skip_gain, out_weight):
    _, rows, channels = features.shape
    own_taps = medium_filter.shape[0]
    short = short_filter.shape[0]
    width = 256
    chunks = channels // width
    edge = 16
    forward, inverse = transforms(rows)
    sizes = (seqs, tps, chunks, width, rows, channels, own_taps, short)
    vmem = pl.BlockSpec(memory_space=pltpu.VMEM)
    anywhere = pl.BlockSpec(memory_space=pl.ANY)
    dma = pltpu.SemaphoreType.DMA
    columns = out_weight.shape[1]
    return pl.pallas_call(
        functools.partial(kernel, sizes),
        out_shape=jax.ShapeDtypeStruct((rows, columns), BF16),
        in_specs=[anywhere, vmem, vmem, vmem, vmem, vmem, anywhere],
        out_specs=vmem,
        scratch_shapes=[
            pltpu.VMEM((chunks, 3, rows, width), BF16),
            pltpu.VMEM((chunks, 3, edge, width), BF16),
            pltpu.VMEM((3, rows + 8, width), F32),
            pltpu.VMEM((2, rows, width), F32),
            pltpu.VMEM((chunks, rows, width), BF16),
            pltpu.VMEM((chunks, rows // 2, width), BF16),
            pltpu.VMEM((chunks, seqs * own_taps, width), BF16),
            pltpu.VMEM((tps, chunks, rows, width), BF16),
            pltpu.VMEM((tps, chunks, width, columns), BF16),
            pltpu.VMEM((rows, columns), F32),
            dma((chunks,)),
            dma((tps, chunks)),
            dma((chunks,)),
            dma((chunks,)),
            dma((chunks,)),
            dma((chunks,)),
            dma((chunks, seqs - 1)),
            dma((chunks, seqs - 1)),
            dma((chunks, 2)),
            dma((chunks, 2)),
            dma((chunks, 2)),
            dma((chunks, 2)),
        ],
        compiler_params=pltpu.CompilerParams(
            collective_id=0, has_side_effects=True, vmem_limit_bytes=56 * 1024 * 1024
        ),
    )(
        features,
        short_filter,
        medium_filter,
        skip_gain.reshape(1, channels),
        jnp.asarray(forward),
        jnp.asarray(inverse),
        out_weight,
    )


def solution(mesh):
    in_specs = (P(None, "seq", "tp"), P(None, None, "tp"), P("seq", "tp"), P("tp"), P(None, "tp"))
    out_specs = P("seq", "tp")
    seqs, tps = mesh.shape["seq"], mesh.shape["tp"]

    def body(features, short_filter, medium_filter, skip_gain, out_weight):
        taps_all = seqs * medium_filter.shape[0]
        fits = (
            tps == 4
            and seqs > 1
            and medium_filter.shape[0] % 16 == 0
            and features.shape[1] == 2 * taps_all
            and features.shape[2] % 512 == 0
            and short_filter.shape[0] <= 9
        )
        if fits:
            return fused(
                seqs, tps, features, short_filter, medium_filter, skip_gain, out_weight
            )
        return on_device(features, short_filter, medium_filter, skip_gain, out_weight)

    return jax.shard_map(body, mesh=mesh, in_specs=in_specs, out_specs=out_specs, check_vma=False)
```

profile of v0, /device:TPU:18, one launch (start us, length us, event | category | flops | bytes accessed | tf_op | source)
XLA Modules:
  0.0 69.3 jit_solution(608022862268556844)
XLA Ops:
  0.0 1.7 %copy.8.short_ref = f32[7,3,2048]{2,1,0:T(4,128)} copy(f32[7,3,2048]{2,0,1:T(8,128)} %param.8) | data formatting | bytes 344064 | tf_op args[1]
  1.7 65.3 %shard_map.73 = bf16[256,2048]{1,0:T(8,128)(2,1)} custom-call(bf16[3,256,2048]{2,1,0:T(8,128)(2,1)} %features.1, f32[7,3,2048]{2,1,0:T(4,128)} %copy.8.short_ref, f32[16,2048]{1,0:T(8,128)} %medium_ref.1, f32[1,2048]{1,0:T(1,128)} %bitcast.1, bf16[2,256,256]{2,1,0:T(8,128)(2,1)} %constant.4.clone.forward_ref, ...), custom_call_target="tpu_custom_call" | custom-call | tf_op jit(solution)/shard_map/pallas_call | solution.py:364
  67.0 2.3 %copy.10 = bf16[256,2048]{1,0:T(8,128)(2,1)} copy(bf16[256,2048]{1,0:T(8,128)(2,1)} %shard_map.73) | data formatting | bytes 2097152
where the time goes:
time: 69.5 us; the launch traced here: 69.3 us
  Pallas kernels  65.3 us (94%)
  local copies, waits for them, and re-layouts  4.04 us (6%)
    pallas_call x1, Pallas kernels, fused(): pl.pallas_call(functools.partial(kernel, sizes), out_shape=jax.ShapeDtype...  65.3 us
    unnamed x2, local copies, waits for them, and re-layouts  4.04 us

commit v1 on v0

--- a/solution.py
+++ b/solution.py
@@ -216,8 +216,7 @@
     acc[...] = jnp.zeros_like(acc)
     pl.semaphore_wait(barrier, seqs + 1)
 
-    @pl.loop(0, chunks)
-    def _(c):
+    def share(c):
         feat_copy(c).wait()
 
         @pl.when(s < seqs - 1)
@@ -226,6 +225,12 @@
 
         for k in range(1, seqs):
             tap_copy(c, k).start()
+
+    ahead = 2
+
+    @pl.loop(0, min(ahead, chunks))
+    def _(c):
+        share(c)
 
     @pl.loop(0, chunks)
     def _(c):
@@ -238,7 +243,7 @@
         ext[stream, 8:, :] = feat[c, stream, :, :].astype(F32)
         total = None
         for j in range(short):
-            term = short_ref[j, pl.ds(stream, 1), lanes] * ext[stream, pl.ds(8 - j, rows), :]
+            term = short_ref[stream, pl.ds(j, 1), lanes] * ext[stream, pl.ds(8 - j, rows), :]
             total = term if total is None else total + term
         return total
 
@@ -298,24 +303,24 @@
 
     tile = 512
 
-    def project(c):
-        for way in range(2):
-            d_copy(across, c, way).wait_recv()
-        for q in range(tps):
+    def project(c, owners):
+        for q in owners:
             w_copy(q, c).wait()
 
         @pl.loop(0, channels // tile)
         def _(n):
             lanes = pl.ds(pl.multiple_of(n * tile, tile), tile)
             total = acc[:, lanes]
-            for q in range(tps):
+            for q in owners:
                 total = total + dot(gath[q, c], wbuf[q, c, :, lanes])
             acc[:, lanes] = total
 
-    lag = 3
-
-    @pl.loop(0, chunks + lag)
+    @pl.loop(0, chunks + 4)
     def _(i):
+        @pl.when(i + ahead < chunks)
+        def _():
+            share(i + ahead)
+
         @pl.when(i < chunks)
         def _():
             products(i)
@@ -324,13 +329,16 @@
         def _():
             gate(i - 1)
 
-        @pl.when((i >= 2) & (i < chunks + 2))
-        def _():
-            pass_on(i - 2)
-
-        @pl.when(i >= lag)
-        def _():
-            project(i - lag)
+        @pl.when((i >= 3) & (i < chunks + 3))
+        def _():
+            pass_on(i - 3)
+            project(i - 3, (p,) + beside)
+
+        @pl.when(i >= 4)
+        def _():
+            for way in range(2):
+                d_copy(across, i - 4, way).wait_recv()
+            project(i - 4, (across,))
 
     out_ref[...] = acc[...].astype(BF16)
 
@@ -395,7 +403,7 @@
         ),
     )(
         features,
-        short_filter,
+        short_filter.transpose(1, 0, 2),
         medium_filter,
         skip_gain.reshape(1, channels),
         jnp.asarray(forward),

time: 69.5 us -> 57.9 us (0.83)
  the two profiles are of different devices: /device:TPU:18 before, /device:TPU:0 now
where the time goes in v1:
time: 57.9 us; the launch traced here: 57.4 us
  Pallas kernels  55.1 us (95%)
  local copies, waits for them, and re-layouts  2.3 us (4%)
    pallas_call x1, Pallas kernels, fused(): pl.pallas_call(functools.partial(kernel, sizes), out_shape=jax.ShapeDtype...  55.1 us
    unnamed x1, local copies, waits for them, and re-layouts  2.3 us

profile of v1, /device:TPU:0, one launch (start us, length us, event | category | flops | bytes accessed | tf_op | source)
XLA Modules:
  0.0 57.4 jit_solution(7618285759592006853)
XLA Ops:
  0.0 55.1 %shard_map.73 = bf16[256,2048]{1,0:T(8,128)(2,1)} custom-call(bf16[3,256,2048]{2,1,0:T(8,128)(2,1)} %features.1, f32[3,7,2048]{2,1,0:T(8,128)} %bitcast.2, f32[16,2048]{1,0:T(8,128)} %medium_ref.1, f32[1,2048]{1,0:T(1,128)} %bitcast.3, bf16[2,256,256]{2,1,0:T(8,128)(2,1)} %constant.4.clone.forward_ref, bf16[2,128,256]{2,1,0:T(8,128)(2,1)} %constant.5.clone.inverse_ref, ...), custom_call_target="tpu_custom_call" | custom-call | tf_op jit(solution)/shard_map/pallas_call | solution.py:372
  55.1 2.3 %copy.9 = bf16[256,2048]{1,0:T(8,128)(2,1)} copy(bf16[256,2048]{1,0:T(8,128)(2,1)} %shard_map.73) | data formatting | bytes 2097152

commit v2 on v1

--- a/solution.py
+++ b/solution.py
@@ -213,12 +213,36 @@
         fhalo[...] = jnp.zeros_like(fhalo)
         phalo[...] = jnp.zeros_like(phalo)
 
-    acc[...] = jnp.zeros_like(acc)
-    pl.semaphore_wait(barrier, seqs + 1)
+    def short_conv(c, stream, start):
+        lanes = pl.ds(pl.multiple_of(c * width, width), width)
+        total = None
+        for j in range(short):
+            piece = ext[stream, pl.ds(start + 8 - j, half), :]
+            term = short_ref[stream, pl.ds(j, 1), lanes] * piece
+            total = term if total is None else total + term
+        return total
+
+    def convolve(c, start):
+        here = pl.ds(start, half)
+        product = short_conv(c, 1, start) * short_conv(c, 2, start)
+        prod[c, here, :] = product.astype(BF16)
+        query[lax.rem(c, 2), here, :] = short_conv(c, 0, start)
+
+    def later(c):
+        for stream in range(3):
+            ext[stream, 8:, :] = feat[c, stream, :, :].astype(F32)
+        convolve(c, half)
+
+    def earlier(c):
+        @pl.when(s > 0)
+        def _():
+            fh_copy(c).wait_recv()
+
+        for stream in range(3):
+            ext[stream, 0:8, :] = fhalo[c, stream, :, :].astype(F32)[edge - 8 :]
+        convolve(c, 0)
 
     def share(c):
-        feat_copy(c).wait()
-
         @pl.when(s < seqs - 1)
         def _():
             fh_copy(c).start()
@@ -226,39 +250,23 @@
         for k in range(1, seqs):
             tap_copy(c, k).start()
 
-    ahead = 2
-
-    @pl.loop(0, min(ahead, chunks))
-    def _(c):
-        share(c)
+    def hand_on(c):
+        @pl.when(s < seqs - 1)
+        def _():
+            ph_copy(c).start()
+
+    feat_copy(0).wait()
+    later(0)
+    pl.semaphore_wait(barrier, seqs + 1)
+    share(0)
+    hand_on(0)
 
     @pl.loop(0, chunks)
     def _(c):
         for q in range(tps):
             w_copy(q, c).start()
 
-    def short_conv(c, stream):
-        lanes = pl.ds(pl.multiple_of(c * width, width), width)
-        ext[stream, 0:8, :] = fhalo[c, stream, :, :].astype(F32)[edge - 8 :]
-        ext[stream, 8:, :] = feat[c, stream, :, :].astype(F32)
-        total = None
-        for j in range(short):
-            term = short_ref[stream, pl.ds(j, 1), lanes] * ext[stream, pl.ds(8 - j, rows), :]
-            total = term if total is None else total + term
-        return total
-
-    def products(c):
-        @pl.when(s > 0)
-        def _():
-            fh_copy(c).wait_recv()
-
-        prod[c] = (short_conv(c, 1) * short_conv(c, 2)).astype(BF16)
-
-        @pl.when(s < seqs - 1)
-        def _():
-            ph_copy(c).start()
-
-        query[lax.rem(c, 2)] = short_conv(c, 0)
+    acc[...] = jnp.zeros_like(acc)
 
     def gate(c):
         lanes = pl.ds(pl.multiple_of(c * width, width), width)
@@ -315,30 +323,36 @@
                 total = total + dot(gath[q, c], wbuf[q, c, :, lanes])
             acc[:, lanes] = total
 
-    @pl.loop(0, chunks + 4)
+    @pl.loop(0, chunks + 3)
     def _(i):
-        @pl.when(i + ahead < chunks)
-        def _():
-            share(i + ahead)
+        @pl.when(i + 1 < chunks)
+        def _():
+            feat_copy(i + 1).wait()
+            share(i + 1)
 
         @pl.when(i < chunks)
         def _():
-            products(i)
-
-        @pl.when((i >= 1) & (i < chunks + 1))
-        def _():
-            gate(i - 1)
-
-        @pl.when((i >= 3) & (i < chunks + 3))
-        def _():
-            pass_on(i - 3)
-            project(i - 3, (p,) + beside)
-
-        @pl.when(i >= 4)
+            earlier(i)
+
+        @pl.when(i + 1 < chunks)
+        def _():
+            later(i + 1)
+            hand_on(i + 1)
+
+        @pl.when(i < chunks)
+        def _():
+            gate(i)
+
+        @pl.when((i >= 2) & (i < chunks + 2))
+        def _():
+            pass_on(i - 2)
+            project(i - 2, (p,) + beside)
+
+        @pl.when(i >= 3)
         def _():
             for way in range(2):
-                d_copy(across, i - 4, way).wait_recv()
-            project(i - 4, (across,))
+                d_copy(across, i - 3, way).wait_recv()
+            project(i - 3, (across,))
 
     out_ref[...] = acc[...].astype(BF16)
 

time: 57.9 us -> 57 us (0.984)
  Pallas kernels: 55.1 us -> 54.5 us
    pallas_call x1, Pallas kernels: 55.1 us -> 54.5 us  [fused(): pl.pallas_call(functools.partial(kernel, sizes), out_shape=jax.ShapeDtype...]
where the time goes in v2:
time: 57 us; the launch traced here: 56.8 us
  Pallas kernels  54.5 us (96%)
  local copies, waits for them, and re-layouts  2.3 us (4%)
    pallas_call x1, Pallas kernels, fused(): pl.pallas_call(functools.partial(kernel, sizes), out_shape=jax.ShapeDtype...  54.5 us
    unnamed x1, local copies, waits for them, and re-layouts  2.3 us

profile of v2, /device:TPU:0, one launch (start us, length us, event | category | flops | bytes accessed | tf_op | source)
XLA Modules:
  0.0 56.8 jit_solution(3301391092803226704)
XLA Ops:
  0.0 54.5 %shard_map.73 = bf16[256,2048]{1,0:T(8,128)(2,1)} custom-call(bf16[3,256,2048]{2,1,0:T(8,128)(2,1)} %features.1, f32[3,7,2048]{2,1,0:T(8,128)} %bitcast.2, f32[16,2048]{1,0:T(8,128)} %medium_ref.1, f32[1,2048]{1,0:T(1,128)} %bitcast.3, bf16[2,256,256]{2,1,0:T(8,128)(2,1)} %constant.4.clone.forward_ref, bf16[2,128,256]{2,1,0:T(8,128)(2,1)} %constant.5.clone.inverse_ref, ...), custom_call_target="tpu_custom_call" | custom-call | tf_op jit(solution)/shard_map/pallas_call | solution.py:386
  54.5 2.3 %copy.9 = bf16[256,2048]{1,0:T(8,128)(2,1)} copy(bf16[256,2048]{1,0:T(8,128)(2,1)} %shard_map.73) | data formatting | bytes 2097152

commit v3 on v2

--- a/solution.py
+++ b/solution.py
@@ -173,12 +173,13 @@
             device_id_type=MESH,
         )
 
-    def g_copy(owner, c, way):
-        return pltpu.make_async_remote_copy(
-            src_ref=gath.at[owner, c],
-            dst_ref=gath.at[owner, c],
-            send_sem=g_send.at[c, way],
-            recv_sem=g_recv.at[c, way],
+    def g_copy(owner, c, way, part):
+        piece = pl.ds(part * half, half)
+        return pltpu.make_async_remote_copy(
+            src_ref=gath.at[owner, c, piece, :],
+            dst_ref=gath.at[owner, c, piece, :],
+            send_sem=g_send.at[c, 2 * way + part],
+            recv_sem=g_recv.at[c, 2 * way + part],
             device_id=(s, beside[way]),
             device_id_type=MESH,
         )
@@ -294,6 +295,8 @@
         slot = lax.rem(c, 2)
         upper = block(prod[c, 0:half, :], prod[c, half:, :])
         gath[p, c, pl.ds(half, half), :] = (query[slot, pl.ds(half, half), :] * upper).astype(BF16)
+        for way in range(2):
+            g_copy(p, c, way, 1).start()
 
         @pl.when(s > 0)
         def _():
@@ -302,14 +305,16 @@
         lower = block(phalo[c], prod[c, 0:half, :])
         gath[p, c, pl.ds(0, half), :] = (query[slot, pl.ds(0, half), :] * lower).astype(BF16)
         for way in range(2):
-            g_copy(p, c, way).start()
+            g_copy(p, c, way, 0).start()
 
     def pass_on(c):
-        for way in range(2):
-            g_copy(beside[way], c, way).wait_recv()
+        for way in (1, 0):
+            g_copy(beside[way], c, way, way).wait_recv()
             d_copy(beside[way], c, way).start()
-
-    tile = 512
+        for way in (0, 1):
+            g_copy(beside[way], c, way, 1 - way).wait_recv()
+
+    tile = 1024
 
     def project(c, owners):
         for q in owners:
@@ -366,7 +371,8 @@
         for k in range(1, seqs):
             tap_copy(c, k).wait_send()
         for way in range(2):
-            g_copy(p, c, way).wait_send()
+            for part in range(2):
+                g_copy(p, c, way, part).wait_send()
             d_copy(beside[way], c, way).wait_send()
 
 
@@ -407,8 +413,8 @@
             dma((chunks,)),
             dma((chunks, seqs - 1)),
             dma((chunks, seqs - 1)),
-            dma((chunks, 2)),
-            dma((chunks, 2)),
+            dma((chunks, 4)),
+            dma((chunks, 4)),
             dma((chunks, 2)),
             dma((chunks, 2)),
         ],
@@ -438,7 +444,7 @@
             and seqs > 1
             and medium_filter.shape[0] % 16 == 0
             and features.shape[1] == 2 * taps_all
-            and features.shape[2] % 512 == 0
+            and features.shape[2] % 1024 == 0
             and short_filter.shape[0] <= 9
         )
         if fits:

time: 57 us -> 55.3 us (0.970)
  Pallas kernels: 54.5 us -> 52.9 us
    pallas_call x1, Pallas kernels: 54.5 us -> 52.9 us  [fused(): pl.pallas_call(functools.partial(kernel, sizes), out_shape=jax.ShapeDtype...]
where the time goes in v3:
time: 55.3 us; the launch traced here: 55.2 us
  Pallas kernels  52.9 us (96%)
  local copies, waits for them, and re-layouts  2.3 us (4%)
    pallas_call x1, Pallas kernels, fused(): pl.pallas_call(functools.partial(kernel, sizes), out_shape=jax.ShapeDtype...  52.9 us
    unnamed x1, local copies, waits for them, and re-layouts  2.3 us

profile of v3, /device:TPU:0, one launch (start us, length us, event | category | flops | bytes accessed | tf_op | source)
XLA Modules:
  0.0 55.2 jit_solution(14737812987425150413)
XLA Ops:
  0.0 52.9 %shard_map.73 = bf16[256,2048]{1,0:T(8,128)(2,1)} custom-call(bf16[3,256,2048]{2,1,0:T(8,128)(2,1)} %features.1, f32[3,7,2048]{2,1,0:T(8,128)} %bitcast.2, f32[16,2048]{1,0:T(8,128)} %medium_ref.1, f32[1,2048]{1,0:T(1,128)} %bitcast.3, bf16[2,256,256]{2,1,0:T(8,128)(2,1)} %constant.4.clone.forward_ref, bf16[2,128,256]{2,1,0:T(8,128)(2,1)} %constant.5.clone.inverse_ref, ...), custom_call_target="tpu_custom_call" | custom-call | tf_op jit(solution)/shard_map/pallas_call | solution.py:392
  52.9 2.3 %copy.9 = bf16[256,2048]{1,0:T(8,128)(2,1)} copy(bf16[256,2048]{1,0:T(8,128)(2,1)} %shard_map.73) | data formatting | bytes 2097152

commit v4 on v3

--- a/solution.py
+++ b/solution.py
@@ -316,7 +316,7 @@
 
     tile = 1024
 
-    def project(c, owners):
+    def project(c, owners, last=False):
         for q in owners:
             w_copy(q, c).wait()
 
@@ -326,7 +326,10 @@
             total = acc[:, lanes]
             for q in owners:
                 total = total + dot(gath[q, c], wbuf[q, c, :, lanes])
-            acc[:, lanes] = total
+            if last:
+                out_ref[:, lanes] = total.astype(BF16)
+            else:
+                acc[:, lanes] = total
 
     @pl.loop(0, chunks + 3)
     def _(i):
@@ -357,9 +360,12 @@
         def _():
             for way in range(2):
                 d_copy(across, i - 3, way).wait_recv()
-            project(i - 3, (across,))
-
-    out_ref[...] = acc[...].astype(BF16)
+
+            @pl.when(i < chunks + 2)
+            def _():
+                project(i - 3, (across,))
+
+    project(chunks - 1, (across,), last=True)
 
     @pl.loop(0, chunks)
     def _(c):

time: 55.3 us -> 55.3 us (level)
  no operation moved by 1% of the time
where the time goes in v4:
time: 55.3 us; the launch traced here: 55.1 us
  Pallas kernels  52.8 us (95%)
  local copies, waits for them, and re-layouts  2.3 us (4%)
    pallas_call x1, Pallas kernels, fused(): pl.pallas_call(functools.partial(kernel, sizes), out_shape=jax.ShapeDtype...  52.8 us
    unnamed x1, local copies, waits for them, and re-layouts  2.3 us

profile of v4, /device:TPU:0, one launch (start us, length us, event | category | flops | bytes accessed | tf_op | source)
XLA Modules:
  0.0 55.1 jit_solution(13796477932066009895)
XLA Ops:
  0.0 52.8 %shard_map.73 = bf16[256,2048]{1,0:T(8,128)(2,1)} custom-call(bf16[3,256,2048]{2,1,0:T(8,128)(2,1)} %features.1, f32[3,7,2048]{2,1,0:T(8,128)} %bitcast.2, f32[16,2048]{1,0:T(8,128)} %medium_ref.1, f32[1,2048]{1,0:T(1,128)} %bitcast.3, bf16[2,256,256]{2,1,0:T(8,128)(2,1)} %constant.4.clone.forward_ref, bf16[2,128,256]{2,1,0:T(8,128)(2,1)} %constant.5.clone.inverse_ref, ...), custom_call_target="tpu_custom_call" | custom-call | tf_op jit(solution)/shard_map/pallas_call | solution.py:398
  52.8 2.3 %copy.9 = bf16[256,2048]{1,0:T(8,128)(2,1)} copy(bf16[256,2048]{1,0:T(8,128)(2,1)} %shard_map.73) | data formatting | bytes 2097152
